TPU v7x, 128 devices: a whole 4x4x4 slice. The times are simulated.
128 devices in a mesh: dp: 32 (over x_hi, z, y), tensor: 4 (over x_lo, core).
Axes of the slice: x: 4 (x_hi: 2, x_lo: 2; x = x_hi * 2 + x_lo), y: 4, z: 4, core: 2. Of those that a mesh axis runs over, the one named last changes fastest.
Arguments:
- tokens: bfloat16 [32768, 640], P(('dp', 'tensor')), may hold values from -6 to 6
- segments: int32 [32, 1024], P('dp'), may hold values from 0 to 2, as said below
- cotangent: bfloat16 [32768, 640], P(('dp', 'tensor')), may hold values from -24 to 24
- w_query: bfloat16 [640, 1024], P('dp', 'tensor'), may hold values from -0.25 to 0.25
- w_keyval: bfloat16 [640, 512], P('dp'), may hold values from -0.25 to 0.25
- w_out: bfloat16 [1024, 640], P('tensor', 'dp'), may hold values from -0.1875 to 0.1875
- w_gate: bfloat16 [640, 2048], P('dp', 'tensor'), may hold values from -0.25 to 0.25
- w_up: bfloat16 [640, 2048], P('dp', 'tensor'), may hold values from -0.25 to 0.25
- w_down: bfloat16 [2048, 640], P('tensor', 'dp'), may hold values from -0.125 to 0.125
- gain_in: float32 [640], replicated, may hold values from 0.25 to 1.75
- gain_post_attn: float32 [640], replicated, may hold values from 0.25 to 1.75
- gain_pre_ff: float32 [640], replicated, may hold values from 0.25 to 1.75
- gain_post_ff: float32 [640], replicated, may hold values from 0.25 to 1.75
- gain_query: float32 [256], replicated, may hold values from 0.25 to 1.75
- gain_key: float32 [256], replicated, may hold values from 0.25 to 1.75
Outputs:
- output: bfloat16 [32768, 640], P(('dp', 'tensor'))
- grad_x: float32 [32768, 640], P(('dp', 'tensor'))
- grad_query: float32 [640, 1024], P('dp', 'tensor')
- grad_keyval: float32 [640, 512], P('dp')
- grad_out: float32 [1024, 640], P('tensor', 'dp')
- grad_gate: float32 [640, 2048], P('dp', 'tensor')
- grad_up: float32 [640, 2048], P('dp', 'tensor')
- grad_down: float32 [2048, 640], P('tensor', 'dp')
- grad_gain_in: float32 [640], replicated
- grad_gain_post_attn: float32 [640], replicated
- grad_gain_pre_ff: float32 [640], replicated
- grad_gain_post_ff: float32 [640], replicated
- grad_gain_query: float32 [256], replicated
- grad_gain_key: float32 [256], replicated
Inputs may be any that keep to these rules, and one draw needn't show every extreme that they name: `segments`: along each row the numbers never fall; each row holds three documents numbered 0, 1, 2, each of one token or more, where document 1 starts within the first 256 tokens and ends within the last 256.
All inputs are finite; a program needn't handle non-finite values.
Results may differ from a plain program's by a relative error of at most 0.024.
Values may be sent and summed in bfloat16 or wider, within the bound.
A program may use at most 128 MiB of HBM per device.

v0:
```python
import jax
import jax.numpy as jnp
from jax import lax
from jax.sharding import PartitionSpec as P

HD = 256
WINDOW = 512
norm_eps = 1e-06
rope_base = 10000.0


def rms_scale(array_in, gain_row):
    return (
        array_in
        * lax.rsqrt(jnp.mean(array_in * array_in, axis=-1, keepdims=True) + norm_eps)
        * gain_row
    )


def rotate_half(array_in):
    half_width = array_in.shape[-1] // 2
    return jnp.concatenate([-array_in[..., half_width:], array_in[..., :half_width]], axis=-1)


def rope_tables(position_ids, head_width):
    inv_freq = rope_base ** (-jnp.arange(0, head_width, 2).astype(jnp.float32) / head_width)
    angles = position_ids.astype(jnp.float32)[:, None] * inv_freq[None, :]
    angles = jnp.concatenate([angles, angles], axis=-1)
    return (jnp.cos(angles), jnp.sin(angles))


def segment_positions(seg_ids):
    row_index = jnp.arange(seg_ids.shape[0], dtype=jnp.int32)
    prev_ids = jnp.concatenate([seg_ids[:1] - 1, seg_ids[:-1]])
    doc_start = lax.cummax(jnp.where(seg_ids != prev_ids, row_index, 0), axis=0)
    return row_index - doc_start


def prepare(raw_rows, gain_row, cos_rows, sin_rows):
    normed = rms_scale(raw_rows, gain_row)
    return normed * cos_rows + rotate_half(normed) * sin_rows


def norm_back(array_in, gain_row, grad_rows):
    _, back_fn = jax.vjp(rms_scale, array_in, gain_row)
    return back_fn(grad_rows)


def gelu_product(gate_rows, up_rows):
    return jax.nn.gelu(gate_rows, approximate=True) * up_rows


def contract_rows(left_rows, right_rows):
    return lax.dot_general(
        left_rows, right_rows, (((0,), (0,)), ((), ())), preferred_element_type=jnp.float32
    )


def project_back(grad_rows, weight_rows):
    return lax.dot_general(
        grad_rows, weight_rows, (((1,), (1,)), ((), ())), preferred_element_type=jnp.float32
    )


def per_device(
    tokens,
    segments,
    cotangent,
    w_query,
    w_keyval,
    w_out,
    w_gate,
    w_up,
    w_down,
    gain_in,
    gain_post_attn,
    gain_pre_ff,
    gain_post_ff,
    gain_query,
    gain_key,
):
    tok_rows = tokens.shape[0]
    seq_rows = tok_rows * lax.axis_size("tensor")
    model_width = tokens.shape[1]
    heads_here = w_query.shape[1] // HD
    seg_ids = segments[0]
    positions = segment_positions(seg_ids)
    cos_rows, sin_rows = rope_tables(positions, HD)
    cos_heads = cos_rows[:, None, :]
    sin_heads = sin_rows[:, None, :]
    score_scale = HD ** (-0.5)
    q_block = min(512, seq_rows)
    key_reach = -(-WINDOW // q_block) * q_block
    key_span = min(seq_rows, q_block + key_reach)
    starts = jnp.arange(seq_rows // q_block, dtype=jnp.int32) * q_block
    x_local = tokens.astype(jnp.float32)
    attn_local = rms_scale(x_local, gain_in).astype(jnp.bfloat16)
    query_full, keyval_full, out_full = (
        lax.all_gather(w_query, "dp", axis=0, tiled=True),
        lax.all_gather(w_keyval, "dp", axis=0, tiled=True),
        lax.all_gather(w_out, "dp", axis=1, tiled=True),
    )
    attn_input = lax.all_gather(attn_local, "tensor", axis=0, tiled=True)
    query_raw = jnp.dot(attn_input, query_full, preferred_element_type=jnp.float32).reshape(
        seq_rows, heads_here, HD
    )
    keyval_raw = jnp.dot(attn_input, keyval_full, preferred_element_type=jnp.float32)
    key_raw = keyval_raw[:, :HD]
    queries = prepare(query_raw, gain_query, cos_heads, sin_heads).astype(jnp.bfloat16)
    key_rows = prepare(key_raw, gain_key, cos_rows, sin_rows).astype(jnp.bfloat16)
    values = keyval_raw[:, HD:].astype(jnp.bfloat16)

    def block_scores(first_row):
        key_start = jnp.clip(first_row - key_reach, 0, seq_rows - key_span)
        query_blk = lax.dynamic_slice_in_dim(queries, first_row, q_block, 0)
        query_index = first_row + jnp.arange(q_block, dtype=jnp.int32)
        key_index = key_start + jnp.arange(key_span, dtype=jnp.int32)
        query_seg = lax.dynamic_slice_in_dim(seg_ids, first_row, q_block, 0)
        offset = query_index[:, None] - key_index[None, :]
        allowed = (query_seg[:, None] == seg_ids[None, :]) & (offset >= 0) & (offset < WINDOW)
        scores = (
            jnp.einsum("qhd,kd->hqk", query_blk, key_rows, preferred_element_type=jnp.float32)
            * score_scale
        )
        scores = jnp.where(allowed[None], scores, -1e30)
        return (scores, query_blk, key_rows, values, key_start)

    def attend(first_row):
        scores, query_blk, key_blk, value_blk, key_start = block_scores(first_row)
        row_max = jnp.max(scores, axis=-1, keepdims=True)
        exp_scores = jnp.exp(scores - row_max)
        exp_sum = jnp.sum(exp_scores, axis=-1, keepdims=True)
        attn_probs = (exp_scores / exp_sum).astype(jnp.bfloat16)
        context_blk = jnp.einsum(
            "hqk,kd->qhd", attn_probs, value_blk, preferred_element_type=jnp.float32
        )
        return (context_blk, (row_max + jnp.log(exp_sum))[..., 0])

    context, log_total = lax.map(attend, starts)
    context_b = context.reshape(seq_rows, heads_here * HD).astype(jnp.bfloat16)
    rows_here = context_b
    attn_proj = lax.psum_scatter(
        jnp.dot(rows_here, out_full, preferred_element_type=jnp.float32),
        "tensor",
        scatter_dimension=0,
        tiled=True,
    )
    mid_rows = x_local + rms_scale(attn_proj, gain_post_attn)
    mlp_local = rms_scale(mid_rows, gain_pre_ff).astype(jnp.bfloat16)
    gate_full, up_full, down_full = (
        lax.all_gather(w_gate, "dp", axis=0, tiled=True),
        lax.all_gather(w_up, "dp", axis=0, tiled=True),
        lax.all_gather(w_down, "dp", axis=1, tiled=True),
    )
    mlp_input = lax.all_gather(mlp_local, "tensor", axis=0, tiled=True)
    gate_rows = jnp.dot(mlp_input, gate_full, preferred_element_type=jnp.float32)
    up_rows = jnp.dot(mlp_input, up_full, preferred_element_type=jnp.float32)
    hidden = gelu_product(gate_rows, up_rows).astype(jnp.bfloat16)
    rows_here = hidden
    mlp_proj = lax.psum_scatter(
        jnp.dot(rows_here, down_full, preferred_element_type=jnp.float32),
        "tensor",
        scatter_dimension=0,
        tiled=True,
    )
    output = (mid_rows + rms_scale(mlp_proj, gain_post_ff)).astype(jnp.bfloat16)
    grad_top = cotangent.astype(jnp.float32)
    d_mlp_f, grad_gain_post_ff = norm_back(mlp_proj, gain_post_ff, grad_top)
    d_mlp_all = lax.all_gather(d_mlp_f.astype(jnp.bfloat16), "tensor", axis=0, tiled=True)
    down_part = contract_rows(hidden, d_mlp_all)
    d_hidden = project_back(d_mlp_all, down_full)
    _, hidden_back = jax.vjp(gelu_product, gate_rows, up_rows)
    d_gate_f, d_up_f = hidden_back(d_hidden)
    d_gate = d_gate_f.astype(jnp.bfloat16)
    d_up = d_up_f.astype(jnp.bfloat16)
    gate_part = contract_rows(mlp_input, d_gate)
    up_part = contract_rows(mlp_input, d_up)
    d_mlp_input = lax.psum_scatter(
        project_back(d_gate, gate_full) + project_back(d_up, up_full),
        "tensor",
        scatter_dimension=0,
        tiled=True,
    )
    grad_gate, grad_up, grad_down = (
        lax.psum_scatter(
            gate_part.astype(jnp.bfloat16), "dp", scatter_dimension=0, tiled=True
        ).astype(jnp.float32),
        lax.psum_scatter(
            up_part.astype(jnp.bfloat16), "dp", scatter_dimension=0, tiled=True
        ).astype(jnp.float32),
        lax.psum_scatter(
            down_part.astype(jnp.bfloat16), "dp", scatter_dimension=1, tiled=True
        ).astype(jnp.float32),
    )
    d_pre, grad_gain_pre_ff = norm_back(mid_rows, gain_pre_ff, d_mlp_input)
    d_mid = grad_top + d_pre
    d_attn_f, grad_gain_post_attn = norm_back(attn_proj, gain_post_attn, d_mid)
    d_attn_all = lax.all_gather(d_attn_f.astype(jnp.bfloat16), "tensor", axis=0, tiled=True)
    out_part = contract_rows(context_b, d_attn_all)
    d_context = (
        project_back(d_attn_all, out_full).astype(jnp.bfloat16).reshape(seq_rows, heads_here, HD)
    )

    def attend_back(carry, inputs):
        d_key_acc, d_value_acc = carry
        first_row, log_rows = inputs
        scores, query_blk, key_blk, value_blk, key_start = block_scores(first_row)
        attn_probs = jnp.exp(scores - log_rows[..., None])
        probs_b = attn_probs.astype(jnp.bfloat16)
        d_context_blk = lax.dynamic_slice_in_dim(d_context, first_row, q_block, 0)
        d_probs = jnp.einsum(
            "qhd,kd->hqk", d_context_blk, value_blk, preferred_element_type=jnp.float32
        )
        d_value_blk = jnp.einsum(
            "hqk,qhd->kd", probs_b, d_context_blk, preferred_element_type=jnp.float32
        )
        row_inner = jnp.sum(attn_probs * d_probs, axis=-1, keepdims=True)
        d_scores = (attn_probs * (d_probs - row_inner)).astype(jnp.bfloat16)
        d_query_blk = (
            jnp.einsum("hqk,kd->qhd", d_scores, key_blk, preferred_element_type=jnp.float32)
            * score_scale
        )
        d_key_blk = (
            jnp.einsum("hqk,qhd->kd", d_scores, query_blk, preferred_element_type=jnp.float32)
            * score_scale
        )
        d_key_acc = d_key_acc + d_key_blk
        d_value_acc = d_value_acc + d_value_blk
        return ((d_key_acc, d_value_acc), d_query_blk)

    zero_rows = jnp.zeros((seq_rows, HD), jnp.float32)
    (d_keys, d_values), d_queries = lax.scan(
        attend_back, (zero_rows, zero_rows), (starts, log_total)
    )
    d_queries = d_queries.reshape(seq_rows, heads_here, HD)

    def query_prepare(raw_rows, gain_row):
        return prepare(raw_rows, gain_row, cos_heads, sin_heads)

    def key_prepare(raw_rows, gain_row):
        return prepare(raw_rows, gain_row, cos_rows, sin_rows)

    _, query_back = jax.vjp(query_prepare, query_raw, gain_query)
    d_query_f, gain_query_part = query_back(d_queries)
    _, key_back = jax.vjp(key_prepare, key_raw, gain_key)
    d_key_f, gain_key_part = key_back(d_keys)
    d_query_b = d_query_f.reshape(seq_rows, heads_here * HD).astype(jnp.bfloat16)
    d_keyval_part = jnp.concatenate([d_key_f, d_values], axis=1)
    summed_back = lax.psum_scatter(
        jnp.concatenate([project_back(d_query_b, query_full), d_keyval_part], axis=1).astype(
            jnp.bfloat16
        ),
        "tensor",
        scatter_dimension=0,
        tiled=True,
    ).astype(jnp.float32)
    d_keyval_b = summed_back[:, model_width:].astype(jnp.bfloat16)
    d_attn_input = summed_back[:, :model_width] + project_back(d_keyval_b, keyval_full)
    query_part = contract_rows(attn_input, d_query_b)
    keyval_part = contract_rows(attn_local, d_keyval_b)
    d_in, gain_in_part = norm_back(x_local, gain_in, d_attn_input)
    grad_x = d_mid + d_in
    grad_query, grad_out = (
        lax.psum_scatter(
            query_part.astype(jnp.bfloat16), "dp", scatter_dimension=0, tiled=True
        ).astype(jnp.float32),
        lax.psum_scatter(
            out_part.astype(jnp.bfloat16), "dp", scatter_dimension=1, tiled=True
        ).astype(jnp.float32),
    )
    shared = lax.psum(
        (
            keyval_part,
            gain_in_part,
            grad_gain_post_attn,
            grad_gain_pre_ff,
            grad_gain_post_ff,
            gain_query_part,
            gain_key_part,
        ),
        ("dp", "tensor"),
    )
    shard_rows = keyval_part.shape[0] // lax.axis_size("dp")
    grad_keyval = lax.dynamic_slice_in_dim(
        shared[0], lax.axis_index("dp") * shard_rows, shard_rows, 0
    )
    return (
        output,
        grad_x,
        grad_query,
        grad_keyval,
        grad_out,
        grad_gate,
        grad_up,
        grad_down,
        shared[1],
        shared[2],
        shared[3],
        shared[4],
        shared[5],
        shared[6],
    )


def solution(mesh):
    return jax.shard_map(
        per_device,
        mesh=mesh,
        in_specs=(
            P(("dp", "tensor"), None),
            P("dp", None),
            P(("dp", "tensor"), None),
            P("dp", "tensor"),
            P("dp", None),
            P("tensor", "dp"),
            P("dp", "tensor"),
            P("dp", "tensor"),
            P("tensor", "dp"),
            P(),
            P(),
            P(),
            P(),
            P(),
            P(),
        ),
        out_specs=(
            P(("dp", "tensor"), None),
            P(("dp", "tensor"), None),
            P("dp", "tensor"),
            P("dp", None),
            P("tensor", "dp"),
            P("dp", "tensor"),
            P("dp", "tensor"),
            P("tensor", "dp"),
            P(),
            P(),
            P(),
            P(),
            P(),
            P(),
        ),
        check_vma=False,
    )
```

profile of v0, /device:TPU:1, one launch (start us, length us, event | category | flops | bytes accessed | tf_op | source)
XLA Modules:
  0.0 1217.1 jit_solution(458349446832109344)
XLA Ops:
  8.4 1.9 fusion.73
  10.3 88.9 %all-gather.1 = bf16[32,20,512]{2,1,0:T(8,128)(2,1)S(1)} all-gather(bf16[1,20,512]{2,1,0:T(8,128)(2,1)} %bitcast.278), channel_id=1, replica_groups=mesh['dp'=32,'tensor'=4] {'dp'}, dimensions={0}, use_global_device_ids=true | all-gather | bytes 675840 | tf_op jit(solution)/shard_map/all_gather | solution.py:100
  99.4 75.5 %all-gather = bf16[32,20,256]{2,1,0:T(8,128)(2,1)S(1)} all-gather(bf16[1,20,256]{2,1,0:T(8,128)(2,1)S(1)} %bitcast.282), channel_id=1, replica_groups=mesh['dp'=32,'tensor'=4] {'dp'}, dimensions={0}, use_global_device_ids=true | all-gather | bytes 337920 | tf_op jit(solution)/shard_map/all_gather | solution.py:99
  176.6 77.2 %all-gather.2 = bf16[32,20,256]{2,1,0:T(8,128)(2,1)S(1)} all-gather(bf16[1,20,256]{2,1,0:T(8,128)(2,1)S(1)} %bitcast.283), channel_id=1, replica_groups=mesh['dp'=32,'tensor'=4] {'dp'}, dimensions={0}, use_global_device_ids=true | all-gather | bytes 337920 | tf_op jit(solution)/shard_map/all_gather | solution.py:101
  255.0 2.5 fusion.103
  261.3 5.5 fusion.60
  270.3 14.0 %while.33 = (s32[]{:T(128)}, bf16[2,512,1,256]{3,1,2,0:T(8,128)(2,1)S(1)}, f32[2,1,512]{2,1,0:T(1,128)S(1)}, s32[2]{0:T(128)S(1)}, s32[1024]{0:T(1024)S(1)}, /*i...) while((s32[]{:T(128)}, ...), condition=%wide.region_8.9_spmd.clone, body=%wide.region_5.8_spmd.sunk.clone | while | flops 544211968 | bytes 8169671 | solution.py:139
  284.3 2.1 fusion.104
  286.6 68.8 %reduce-scatter.15.cloned.1.call-done = f32[256,640]{1,0:T(8,128)} async-done(((f32[1024,640]{1,0:T(8,128)}), f32[256,640]{1,0:T(8,128)}) %reduce-scatter.15.cloned.1.call-update) | async-done | bytes 655376 | tf_op jit(solution)/shard_map/reduce_scatter | solution.py:142
  358.9 85.7 %all-gather.3 = bf16[32,20,512]{2,1,0:T(8,128)(2,1)S(1)} all-gather(bf16[1,20,512]{2,1,0:T(8,128)(2,1)S(1)} %bitcast.279), channel_id=1, replica_groups=mesh['dp'=32,'tensor'=4] {'dp'}, dimensions={0}, use_global_device_ids=true | all-gather | bytes 675840 | tf_op jit(solution)/shard_map/all_gather | solution.py:151
  444.8 77.7 %all-gather.4 = bf16[32,20,512]{2,1,0:T(8,128)(2,1)S(1)} all-gather(bf16[1,20,512]{2,1,0:T(8,128)(2,1)S(1)} %bitcast.280), channel_id=1, replica_groups=mesh['dp'=32,'tensor'=4] {'dp'}, dimensions={0}, use_global_device_ids=true | all-gather | bytes 675840 | tf_op jit(solution)/shard_map/all_gather | solution.py:152
  523.5 80.3 %all-gather.5 = bf16[32,20,512]{2,1,0:T(8,128)(2,1)S(1)} all-gather(bf16[1,20,512]{2,1,0:T(8,128)(2,1)S(1)} %bitcast.281), channel_id=1, replica_groups=mesh['dp'=32,'tensor'=4] {'dp'}, dimensions={0}, use_global_device_ids=true | all-gather | bytes 675840 | tf_op jit(solution)/shard_map/all_gather | solution.py:153
  604.8 2.4 fusion.105
  607.2 2.6 multiply_convert_fusion.1
  610.9 2.5 fusion.106
  613.5 67.7 %reduce-scatter.17.cloned.1.call-done = f32[256,640]{1,0:T(8,128)} async-done(((f32[1024,640]{1,0:T(8,128)}), f32[256,640]{1,0:T(8,128)}) %reduce-scatter.17.cloned.1.call-update) | async-done | bytes 655376 | tf_op jit(solution)/shard_map/reduce_scatter | solution.py:160
  685.0 11.4 reduce-scatter.19.cloned.1.call-start
  696.3 12.5 %all-gather.15.cloned.1.call-done = bf16[1024,640]{1,0:T(8,128)(2,1)} async-done(((bf16[256,640]{1,0:T(8,128)(2,1)}), bf16[1024,640]{1,0:T(8,128)(2,1)}) %all-gather.15.cloned.1.call-update) | async-done | bytes 1310736 | tf_op jit(solution)/shard_map/all_gather | solution.py:169
  708.9 5.2 multiply_convert_fusion
  715.6 2.5 convolution_add_fusion.1
  718.3 33.4 %reduce-scatter.19.cloned.1.call-done = f32[256,640]{1,0:T(8,128)} async-done(((f32[1024,640]{1,0:T(8,128)}), f32[256,640]{1,0:T(8,128)}) %reduce-scatter.19.cloned.1.call-update) | async-done | bytes 655376 | tf_op jit(solution)/shard_map/reduce_scatter | solution.py:178
  755.5 23.8 %all-gather.17.cloned.1.call-done = bf16[1024,640]{1,0:T(8,128)(2,1)} async-done(((bf16[256,640]{1,0:T(8,128)(2,1)}), bf16[1024,640]{1,0:T(8,128)(2,1)}) %all-gather.17.cloned.1.call-update) | async-done | bytes 1310736 | tf_op jit(solution)/shard_map/all_gather | solution.py:198
  779.3 2.8 fusion.46
  782.1 36.4 %while.34 = (s32[]{:T(128)}, f32[1024,256]{1,0:T(8,128)}, f32[1024,256]{1,0:T(8,128)}, f32[2,512,1,256]{3,1,2,0:T(8,128)}, s32[2]{0:T(128)S(1)}, /*index=5*/s32[...) while((s32[]{:T(128)}, f32[1024,256]{1,0:T(8,128)}, ...), condition=%wide.region_20.21_spmd.clone.clone, body=%wide.region_18.20_spmd.clone.sunk.clone | while | flops 1351484416 | bytes 46170532 | solution.py:232
  784.7 2.9 fusion.204
  789.1 3.0 fusion.205
  792.4 2.5 fusion.207
  797.4 2.5 convolution_add_fusion.5
  802.6 2.9 fusion.204
  807.0 3.0 fusion.205
  810.2 2.9 fusion.207
  815.6 2.9 convolution_add_fusion.5
  818.5 1.6 copy.64
  820.2 3.5 fusion.64
  823.7 4.1 fusion.67
  828.8 1.7 convolution_convert_fusion
  830.9 3.5 fusion.54
  834.5 4.1 multiply_reduce_fusion
  840.4 1.7 pad_maximum_fusion
  843.3 2.3 convolution_convert_fusion.1
  850.3 103.2 %fusion.97 = (bf16[24,256]{1,0:T(8,128)(2,1)S(1)}, bf16[256,24]{0,1:T(8,128)(2,1)S(1)}, bf16[24,512]{1,0:T(8,128)(2,1)S(1)}, bf16[24,512]{1,0:T(8,128)(2,1)S(1)}, bf16[512,24]{0,1:T(8,128)(2,1)S(1)}) fusion(bf16[640,256]{1,0:T(8,128)(2,1)S(1)} %convolution_convert_fusion.6, bf16[256,640]{0,1:T(8,128)(2,1)S(1)} %convolution_convert_fusion.5, ...), kind=kCustom, calls=%all-reduce-scatter.5 | all-reduce-scatter fusion | flops 1572865 | bytes 2720256
  956.1 5.0 collective-permute-start.17
  961.1 1.9 collective-permute-start.11
  963.0 4.8 collective-permute-start.5
  969.2 6.3 collective-permute-start.6
  975.5 3.2 collective-permute-start.7
  978.7 2.3 collective-permute-start.8
  981.0 5.3 collective-permute-start.9
  986.3 3.1 collective-permute-start
  989.4 2.5 collective-permute-start.1
  991.9 4.9 collective-permute-start.2
  996.8 1.9 collective-permute-start.3
  998.8 2.2 collective-permute-start.4
  1002.6 5.2 collective-permute-start.25
  1010.8 1.6 collective-permute-start.28
  1014.6 2.2 collective-permute-start.18
  1016.8 4.6 collective-permute-start.19
  1024.4 1.7 collective-permute-start.22
  1029.1 4.6 collective-permute-start.13
  1033.7 1.9 collective-permute-start.14
  1043.6 2.4 fusion.85
  1046.1 1.7 fusion.74
  1047.7 82.1 %all-reduce.14 = (f32[640]{0:T(1024)}, f32[640]{0:T(1024)}, f32[640]{0:T(1024)}, f32[640]{0:T(1024)}, f32[256]{0:T(256)}, /*index=5*/f32[256]{0:T(256)}) all-reduce(f32[640]{0:T(1024)S(1)} %get-tuple-element.396, f32[640]{0:T(1024)S(1)} %get-tuple-element.392, ...), channel_id=1, replica_groups=mesh['dp'=32,'tensor'=4] {'dp','tensor'}, use_global_device_ids=true, to_apply=%region_32.33 | all-reduce | flops 3072 | bytes 24576 | tf_op jit(solution)/shard_map/psum | solution.py:271
  1130.8 77.9 %all-reduce.18.cloned.1.call-done = f32[640,512]{1,0:T(8,128)} async-done(((f32[640,512]{1,0:T(8,128)}), f32[640,512]{1,0:T(8,128)}) %all-reduce.18.cloned.1.call-update) | async-done | bytes 1310736 | tf_op jit(solution)/shard_map/psum | solution.py:271
  (310 shorter events, 79.1 us)
Async XLA Ops:
  7.2 92.2 %copy-start.55 = (bf16[20,256]{1,0:T(8,128)(2,1)S(1)}, bf16[20,256]{1,0:T(8,128)(2,1)}, u32[]{:S(2)}) copy-start(bf16[20,256]{1,0:T(8,128)(2,1)} %param.22) | copy-start | bytes 30724
  7.2 247.9 %all-gather.11.cloned.1.call-start = ((), (), s32[]{:S(2)}) async-start(), calls=%async_computation.4 | async-start | bytes 1638400 | tf_op jit(solution)/shard_map/all_gather | solution.py:103
  8.4 166.5 %copy-start.45 = (s32[1,1024]{1,0:T(1,128)S(1)}, s32[1,1024]{1,0:T(1,128)}, u32[]{:S(2)}) copy-start(s32[1,1024]{1,0:T(1,128)} %param.20) | copy-start | bytes 12292
  8.4 168.2 %copy-start.56 = (bf16[256,20]{0,1:T(8,128)(2,1)S(1)}, bf16[256,20]{0,1:T(8,128)(2,1)}, u32[]{:S(2)}) copy-start(bf16[256,20]{0,1:T(8,128)(2,1)} %param.24) | copy-start | bytes 30724
  10.3 345.1 %reduce-scatter.15.cloned.1.call-start = ((), (), s32[]{:S(2)}) async-start(), calls=%async_computation.5 | async-start | bytes 3276800 | tf_op jit(solution)/shard_map/reduce_scatter | solution.py:142
  99.3 158.2 %copy-start.24 = (bf16[640,512]{1,0:T(8,128)(2,1)}, bf16[640,512]{1,0:T(8,128)(2,1)S(1)}, u32[]{:S(2)}) copy-start(bf16[640,512]{1,0:T(8,128)(2,1)S(1)} %reshape.726) | copy-start | bytes 1966084
  174.9 83.2 %copy-start.21 = (bf16[640,256]{1,0:T(8,128)(2,1)}, bf16[640,256]{1,0:T(8,128)(2,1)S(1)}, u32[]{:S(2)}) copy-start(bf16[640,256]{1,0:T(8,128)(2,1)S(1)} %reshape.724) | copy-start | bytes 983044
  253.8 30.5 %copy-start.23 = (bf16[640,256]{1,0:T(8,128)(2,1)}, bf16[640,256]{1,0:T(8,128)(2,1)S(1)}, u32[]{:S(2)}) copy-start(bf16[640,256]{1,0:T(8,128)(2,1)S(1)} %reshape.728) | copy-start | bytes 983044
  255.0 5.6 copy-start.7
  286.4 70.1 %copy-start.17 = (bf16[256,640]{1,0:T(8,128)(2,1)S(1)}, bf16[256,640]{1,0:T(8,128)(2,1)}, u32[]{:S(2)}) copy-start(bf16[256,640]{1,0:T(8,128)(2,1)} %param.19) | copy-start | bytes 983044
  286.5 70.1 %copy-start.47 = (f32[640]{0:T(1024)S(1)}, f32[640]{0:T(1024)}, u32[]{:S(2)}) copy-start(f32[640]{0:T(1024)} %param.29) | copy-start | bytes 7684
  286.5 71.5 %copy-start.46 = (f32[640]{0:T(1024)S(1)}, f32[640]{0:T(1024)}, u32[]{:S(2)}) copy-start(f32[640]{0:T(1024)} %param.30) | copy-start | bytes 7684
  286.5 72.4 %copy-start.48 = (bf16[20,512]{1,0:T(8,128)(2,1)S(1)}, bf16[20,512]{1,0:T(8,128)(2,1)}, u32[]{:S(2)}) copy-start(bf16[20,512]{1,0:T(8,128)(2,1)} %param.25) | copy-start | bytes 61444
  286.5 318.3 %all-gather.13.cloned.1.call-start = ((), (), s32[]{:S(2)}) async-start(), calls=%async_computation.6 | async-start | bytes 1638400 | tf_op jit(solution)/shard_map/all_gather | solution.py:155
  358.0 86.8 %copy-start.49 = (bf16[20,512]{1,0:T(8,128)(2,1)S(1)}, bf16[20,512]{1,0:T(8,128)(2,1)}, u32[]{:S(2)}) copy-start(bf16[20,512]{1,0:T(8,128)(2,1)} %param.26) | copy-start | bytes 61444
  358.9 322.3 %reduce-scatter.17.cloned.1.call-start = ((), (), s32[]{:S(2)}) async-start(), calls=%async_computation.7 | async-start | bytes 3276800 | tf_op jit(solution)/shard_map/reduce_scatter | solution.py:160
  358.9 164.5 %copy-start.50 = (bf16[512,20]{0,1:T(8,128)(2,1)S(1)}, bf16[512,20]{0,1:T(8,128)(2,1)}, u32[]{:S(2)}) copy-start(bf16[512,20]{0,1:T(8,128)(2,1)} %param.27) | copy-start | bytes 61444
  613.4 69.1 %copy-start.20 = (bf16[256,640]{1,0:T(8,128)(2,1)S(1)}, bf16[256,640]{1,0:T(8,128)(2,1)}, u32[]{:S(2)}) copy-start(bf16[256,640]{1,0:T(8,128)(2,1)} %param.21) | copy-start | bytes 983044
  613.4 69.1 %copy-start.51 = (f32[640]{0:T(1024)S(1)}, f32[640]{0:T(1024)}, u32[]{:S(2)}) copy-start(f32[640]{0:T(1024)} %param.31) | copy-start | bytes 7684
  613.4 95.4 %all-gather.15.cloned.1.call-start = ((), (), s32[]{:S(2)}) async-start(), calls=%async_computation.8 | async-start | bytes 1638400 | tf_op jit(solution)/shard_map/all_gather | solution.py:169
  685.0 66.7 %reduce-scatter.19.cloned.1.call-start = ((), (), s32[]{:S(2)}) async-start(), calls=%async_computation.9 | async-start | bytes 3276800 | tf_op jit(solution)/shard_map/reduce_scatter | solution.py:178
  718.2 34.7 %copy-start.6 = (f32[256,640]{1,0:T(8,128)S(1)}, f32[256,640]{1,0:T(8,128)}, u32[]{:S(2)}) copy-start(f32[256,640]{1,0:T(8,128)} %reduce-scatter.15.cloned.1.call-done) | copy-start | bytes 1966084
  718.2 61.1 %all-gather.17.cloned.1.call-start = ((), (), s32[]{:S(2)}) async-start(), calls=%async_computation.10 | async-start | bytes 1638400 | tf_op jit(solution)/shard_map/all_gather | solution.py:198
  754.4 27.7 %copy-start.11 = (f32[256,640]{1,0:T(8,128)}, f32[256,640]{1,0:T(8,128)S(1)}, u32[]{:S(2)}) copy-start(f32[256,640]{1,0:T(8,128)S(1)} %get-tuple-element.458) | copy-start | bytes 1966084
  754.4 27.7 %copy-start.43 = (bf16[1024,256]{1,0:T(8,128)(2,1)S(1)}, bf16[1024,256]{1,0:T(8,128)(2,1)}, u32[]{:S(2)}) copy-start(bf16[1024,256]{1,0:T(8,128)(2,1)} %copy-done.42) | copy-start | bytes 1572868
  755.4 288.2 %reduce-scatter.21.cloned.1.call-start = ((), (), s32[]{:S(2)}) async-start(), calls=%async_computation.11 | async-start | bytes 2949120 | tf_op jit(solution)/shard_map/reduce_scatter | solution.py:249
  782.1 10.0 copy-start.9
  800.0 10.0 copy-start.9
  842.1 366.7 %all-reduce.18.cloned.1.call-start = ((), (), s32[]{:S(2)}) async-start(), calls=%async_computation.12 | async-start | bytes 2621440 | tf_op jit(solution)/shard_map/psum | solution.py:271
  849.7 162.8 %copy-start.57 = (u32[128]{0:T(128)S(1)}, u32[128]{0:T(128)}, u32[]{:S(2)}) copy-start(u32[128]{0:T(128)} %constant.192) | copy-start | bytes 1540
  850.3 193.4 %copy-start.19 = (bf16[256,640]{1,0:T(8,128)(2,1)S(1)}, bf16[256,640]{1,0:T(8,128)(2,1)}, u32[]{:S(2)}) copy-start(bf16[256,640]{1,0:T(8,128)(2,1)} %fusion.73) | copy-start | bytes 983044
  953.5 22.0 %collective-permute-start.29 = (bf16[512,4]{0,1:T(4,128)(2,1)S(1)}, bf16[512,4]{0,1:T(4,128)(2,1)S(1)}, u32[]{:S(2)}, u32[]{:S(2)}) collective-permute-start(bf16[512,4]{0,1:T(4,128)(2,1)S(1)} %slice.73), channel_id=1, source_target_pairs={{0,24},{4,28},{8,32},{12,36},{16,40},{20,44},{24,48},{28,52},{32,5... | collective-permute-start | bytes 12296
  954.8 23.8 %collective-permute-start.23 = (bf16[4,512]{1,0:T(4,128)(2,1)S(1)}, bf16[4,512]{1,0:T(4,128)(2,1)S(1)}, u32[]{:S(2)}, u32[]{:S(2)}) collective-permute-start(bf16[4,512]{1,0:T(4,128)(2,1)S(1)} %slice.72), channel_id=1, source_target_pairs={{0,24},{4,28},{8,32},{12,36},{16,40},{20,44},{24,48},{28,52},{32,5... | collective-permute-start | bytes 12296
  956.1 24.8 %collective-permute-start.17 = (bf16[4,512]{1,0:T(4,128)(2,1)S(1)}, bf16[4,512]{1,0:T(4,128)(2,1)S(1)}, u32[]{:S(2)}, u32[]{:S(2)}) collective-permute-start(bf16[4,512]{1,0:T(4,128)(2,1)S(1)} %slice.71), channel_id=1, source_target_pairs={{0,24},{4,28},{8,32},{12,36},{16,40},{20,44},{24,48},{28,52},{32,5... | collective-permute-start | bytes 12296
  961.1 6.7 collective-permute-start.11
  963.0 6.1 collective-permute-start.5
  967.9 18.4 %collective-permute-start.10 = (bf16[256,24]{0,1:T(8,128)(2,1)S(1)}, bf16[256,24]{0,1:T(8,128)(2,1)S(1)}, u32[]{:S(2)}, u32[]{:S(2)}) collective-permute-start(bf16[256,24]{0,1:T(8,128)(2,1)S(1)} %get-tuple-element.452), channel_id=1, source_target_pairs={{0,20},{4,24},{8,28},{12,32},{16,36},{20,40},{24,44},{28,48},{32,5... | collective-permute-start | bytes 36872
  969.2 20.2 %collective-permute-start.6 = (bf16[256,24]{0,1:T(8,128)(2,1)S(1)}, bf16[256,24]{0,1:T(8,128)(2,1)S(1)}, u32[]{:S(2)}, u32[]{:S(2)}) collective-permute-start(bf16[256,24]{0,1:T(8,128)(2,1)S(1)} %get-tuple-element.452), channel_id=1, source_target_pairs={{0,4},{4,8},{8,12},{12,16},{16,20},{20,24},{24,28},{28,32},{32,36}... | collective-permute-start | bytes 36872
  975.5 16.4 %collective-permute-start.7 = (bf16[256,24]{0,1:T(8,128)(2,1)S(1)}, bf16[256,24]{0,1:T(8,128)(2,1)S(1)}, u32[]{:S(2)}, u32[]{:S(2)}) collective-permute-start(bf16[256,24]{0,1:T(8,128)(2,1)S(1)} %get-tuple-element.452), channel_id=1, source_target_pairs={{0,8},{4,12},{8,16},{12,20},{16,24},{20,28},{24,32},{28,36},{32,40... | collective-permute-start | bytes 36872
  978.7 18.2 %collective-permute-start.8 = (bf16[256,24]{0,1:T(8,128)(2,1)S(1)}, bf16[256,24]{0,1:T(8,128)(2,1)S(1)}, u32[]{:S(2)}, u32[]{:S(2)}) collective-permute-start(bf16[256,24]{0,1:T(8,128)(2,1)S(1)} %get-tuple-element.452), channel_id=1, source_target_pairs={{0,12},{4,16},{8,20},{12,24},{16,28},{20,32},{24,36},{28,40},{32,4... | collective-permute-start | bytes 36872
  981.0 17.8 %collective-permute-start.9 = (bf16[256,24]{0,1:T(8,128)(2,1)S(1)}, bf16[256,24]{0,1:T(8,128)(2,1)S(1)}, u32[]{:S(2)}, u32[]{:S(2)}) collective-permute-start(bf16[256,24]{0,1:T(8,128)(2,1)S(1)} %get-tuple-element.452), channel_id=1, source_target_pairs={{0,16},{4,20},{8,24},{12,28},{16,32},{20,36},{24,40},{28,44},{32,4... | collective-permute-start | bytes 36872
  986.3 14.7 %collective-permute-start = (bf16[24,256]{1,0:T(8,128)(2,1)S(1)}, bf16[24,256]{1,0:T(8,128)(2,1)S(1)}, u32[]{:S(2)}, u32[]{:S(2)}) collective-permute-start(bf16[24,256]{1,0:T(8,128)(2,1)S(1)} %get-tuple-element.451), channel_id=1, source_target_pairs={{0,4},{4,8},{8,12},{12,16},{16,20},{20,24},{24,28},{28,32},{32,36}... | collective-permute-start | bytes 36872
  989.4 13.2 %collective-permute-start.1 = (bf16[24,256]{1,0:T(8,128)(2,1)S(1)}, bf16[24,256]{1,0:T(8,128)(2,1)S(1)}, u32[]{:S(2)}, u32[]{:S(2)}) collective-permute-start(bf16[24,256]{1,0:T(8,128)(2,1)S(1)} %get-tuple-element.451), channel_id=1, source_target_pairs={{0,8},{4,12},{8,16},{12,20},{16,24},{20,28},{24,32},{28,36},{32,40... | collective-permute-start | bytes 36872
  991.9 16.0 %collective-permute-start.2 = (bf16[24,256]{1,0:T(8,128)(2,1)S(1)}, bf16[24,256]{1,0:T(8,128)(2,1)S(1)}, u32[]{:S(2)}, u32[]{:S(2)}) collective-permute-start(bf16[24,256]{1,0:T(8,128)(2,1)S(1)} %get-tuple-element.451), channel_id=1, source_target_pairs={{0,12},{4,16},{8,20},{12,24},{16,28},{20,32},{24,36},{28,40},{32,4... | collective-permute-start | bytes 36872
  996.8 12.4 %collective-permute-start.3 = (bf16[24,256]{1,0:T(8,128)(2,1)S(1)}, bf16[24,256]{1,0:T(8,128)(2,1)S(1)}, u32[]{:S(2)}, u32[]{:S(2)}) collective-permute-start(bf16[24,256]{1,0:T(8,128)(2,1)S(1)} %get-tuple-element.451), channel_id=1, source_target_pairs={{0,16},{4,20},{8,24},{12,28},{16,32},{20,36},{24,40},{28,44},{32,4... | collective-permute-start | bytes 36872
  998.8 12.0 collective-permute-start.4
  1001.0 13.6 %collective-permute-start.24 = (bf16[512,24]{0,1:T(8,128)(2,1)S(1)}, bf16[512,24]{0,1:T(8,128)(2,1)S(1)}, u32[]{:S(2)}, u32[]{:S(2)}) collective-permute-start(bf16[512,24]{0,1:T(8,128)(2,1)S(1)} %get-tuple-element.455), channel_id=1, source_target_pairs={{0,4},{4,8},{8,12},{12,16},{16,20},{20,24},{24,28},{28,32},{32,36}... | collective-permute-start | bytes 73736
  1002.6 14.2 %collective-permute-start.25 = (bf16[512,24]{0,1:T(8,128)(2,1)S(1)}, bf16[512,24]{0,1:T(8,128)(2,1)S(1)}, u32[]{:S(2)}, u32[]{:S(2)}) collective-permute-start(bf16[512,24]{0,1:T(8,128)(2,1)S(1)} %get-tuple-element.455), channel_id=1, source_target_pairs={{0,8},{4,12},{8,16},{12,20},{16,24},{20,28},{24,32},{28,36},{32,40... | collective-permute-start | bytes 73736
  1007.9 13.6 %collective-permute-start.26 = (bf16[512,24]{0,1:T(8,128)(2,1)S(1)}, bf16[512,24]{0,1:T(8,128)(2,1)S(1)}, u32[]{:S(2)}, u32[]{:S(2)}) collective-permute-start(bf16[512,24]{0,1:T(8,128)(2,1)S(1)} %get-tuple-element.455), channel_id=1, source_target_pairs={{0,12},{4,16},{8,20},{12,24},{16,28},{20,32},{24,36},{28,40},{32,4... | collective-permute-start | bytes 73736
  1009.2 13.8 %collective-permute-start.27 = (bf16[512,24]{0,1:T(8,128)(2,1)S(1)}, bf16[512,24]{0,1:T(8,128)(2,1)S(1)}, u32[]{:S(2)}, u32[]{:S(2)}) collective-permute-start(bf16[512,24]{0,1:T(8,128)(2,1)S(1)} %get-tuple-element.455), channel_id=1, source_target_pairs={{0,16},{4,20},{8,24},{12,28},{16,32},{20,36},{24,40},{28,44},{32,4... | collective-permute-start | bytes 73736
  1010.8 13.5 %collective-permute-start.28 = (bf16[512,24]{0,1:T(8,128)(2,1)S(1)}, bf16[512,24]{0,1:T(8,128)(2,1)S(1)}, u32[]{:S(2)}, u32[]{:S(2)}) collective-permute-start(bf16[512,24]{0,1:T(8,128)(2,1)S(1)} %get-tuple-element.455), channel_id=1, source_target_pairs={{0,20},{4,24},{8,28},{12,32},{16,36},{20,40},{24,44},{28,48},{32,5... | collective-permute-start | bytes 73736
  1014.6 12.9 %collective-permute-start.18 = (bf16[24,512]{1,0:T(8,128)(2,1)S(1)}, bf16[24,512]{1,0:T(8,128)(2,1)S(1)}, u32[]{:S(2)}, u32[]{:S(2)}) collective-permute-start(bf16[24,512]{1,0:T(8,128)(2,1)S(1)} %get-tuple-element.454), channel_id=1, source_target_pairs={{0,4},{4,8},{8,12},{12,16},{16,20},{20,24},{24,28},{28,32},{32,36}... | collective-permute-start | bytes 73736
  1016.8 12.3 %collective-permute-start.19 = (bf16[24,512]{1,0:T(8,128)(2,1)S(1)}, bf16[24,512]{1,0:T(8,128)(2,1)S(1)}, u32[]{:S(2)}, u32[]{:S(2)}) collective-permute-start(bf16[24,512]{1,0:T(8,128)(2,1)S(1)} %get-tuple-element.454), channel_id=1, source_target_pairs={{0,8},{4,12},{8,16},{12,20},{16,24},{20,28},{24,32},{28,36},{32,40... | collective-permute-start | bytes 73736
  1021.5 12.3 %collective-permute-start.20 = (bf16[24,512]{1,0:T(8,128)(2,1)S(1)}, bf16[24,512]{1,0:T(8,128)(2,1)S(1)}, u32[]{:S(2)}, u32[]{:S(2)}) collective-permute-start(bf16[24,512]{1,0:T(8,128)(2,1)S(1)} %get-tuple-element.454), channel_id=1, source_target_pairs={{0,12},{4,16},{8,20},{12,24},{16,28},{20,32},{24,36},{28,40},{32,4... | collective-permute-start | bytes 73736
  1023.1 12.6 %collective-permute-start.21 = (bf16[24,512]{1,0:T(8,128)(2,1)S(1)}, bf16[24,512]{1,0:T(8,128)(2,1)S(1)}, u32[]{:S(2)}, u32[]{:S(2)}) collective-permute-start(bf16[24,512]{1,0:T(8,128)(2,1)S(1)} %get-tuple-element.454), channel_id=1, source_target_pairs={{0,16},{4,20},{8,24},{12,28},{16,32},{20,36},{24,40},{28,44},{32,4... | collective-permute-start | bytes 73736
  1024.4 12.6 %collective-permute-start.22 = (bf16[24,512]{1,0:T(8,128)(2,1)S(1)}, bf16[24,512]{1,0:T(8,128)(2,1)S(1)}, u32[]{:S(2)}, u32[]{:S(2)}) collective-permute-start(bf16[24,512]{1,0:T(8,128)(2,1)S(1)} %get-tuple-element.454), channel_id=1, source_target_pairs={{0,20},{4,24},{8,28},{12,32},{16,36},{20,40},{24,44},{28,48},{32,5... | collective-permute-start | bytes 73736
  1027.5 13.3 %collective-permute-start.12 = (bf16[24,512]{1,0:T(8,128)(2,1)S(1)}, bf16[24,512]{1,0:T(8,128)(2,1)S(1)}, u32[]{:S(2)}, u32[]{:S(2)}) collective-permute-start(bf16[24,512]{1,0:T(8,128)(2,1)S(1)} %get-tuple-element.453), channel_id=1, source_target_pairs={{0,4},{4,8},{8,12},{12,16},{16,20},{20,24},{24,28},{28,32},{32,36}... | collective-permute-start | bytes 73736
  1029.1 11.7 collective-permute-start.13
  1033.7 7.1 collective-permute-start.14
  1035.7 5.1 collective-permute-start.15
  1037.0 3.8 collective-permute-start.16
  1039.8 6.2 copy-start.25
  1039.8 6.2 copy-start.52
  1046.0 83.8 %copy-start.12 = (f32[256,640]{1,0:T(8,128)S(1)}, f32[256,640]{1,0:T(8,128)}, u32[]{:S(2)}) copy-start(f32[256,640]{1,0:T(8,128)} %copy-done.11) | copy-start | bytes 1966084
  (42 other events, 90.1 us)
Sparse Core Ops, SparseCore 0:
  10.4 27.1 all-gather.10
  286.6 68.7 reduce-scatter.14
  359.0 24.7 all-gather.12
  613.5 67.5 reduce-scatter.16
  685.1 23.7 all-gather.14
  718.3 33.2 reduce-scatter.18
  755.5 23.7 all-gather.16
  842.2 35.8 reduce-scatter.20
  1046.2 162.5 all-reduce.17
where the time goes:
time: 1230 us; the launch traced here: 1220 us
  blocking collectives  670 us (54%)
  waiting for transfers between devices  284 us (23%)
  starting transfers between devices  92.6 us (8%)
  matrix products  65.9 us (5%)
  other arithmetic  48.6 us (4%)
  local copies, waits for them, and re-layouts  27.5 us (2%)
  between operations  17 us (1%)
    unnamed x1, blocking collectives  103 us
    all_gather x1, blocking collectives, per_device(): lax.all_gather(w_keyval, 'dp', axis=0, tiled=True)  88.9 us
    all_gather x1, blocking collectives, per_device(): lax.all_gather(w_gate, 'dp', axis=0, tiled=True)  85.7 us
    psum x1, blocking collectives, per_device(): lax.psum((keyval_part, gain_in_part, grad_gain_post_attn, grad_gain_pre_f...  82.1 us
    unnamed x30, starting transfers between devices  80.8 us
    all_gather x1, blocking collectives, per_device(): lax.all_gather(w_down, 'dp', axis=1, tiled=True)  80.3 us
    psum x1, waiting for transfers between devices, per_device(): lax.psum((keyval_part, gain_in_part, grad_gain_post_attn, grad_gain_pre_f...  77.9 us
    all_gather x1, blocking collectives, per_device(): lax.all_gather(w_up, 'dp', axis=0, tiled=True)  77.7 us
  transfers between devices with their start and end apart: 39, of which 6 were waited for; matrix products, arithmetic and copies ran while one was open for 10% of the time, Pallas kernels for 0%

commit v1 on v0

--- a/solution.py
+++ b/solution.py
@@ -98,7 +98,9 @@
     query_full, keyval_full, out_full = (
         lax.all_gather(w_query, "dp", axis=0, tiled=True),
         lax.all_gather(w_keyval, "dp", axis=0, tiled=True),
-        lax.all_gather(w_out, "dp", axis=1, tiled=True),
+        jnp.concatenate(
+            lax.all_to_all(jnp.stack([w_out] * lax.axis_size("dp")), "dp", 0, 0), axis=1
+        ),
     )
     attn_input = lax.all_gather(attn_local, "tensor", axis=0, tiled=True)
     query_raw = jnp.dot(attn_input, query_full, preferred_element_type=jnp.float32).reshape(

time: 1230 us -> 1150 us (0.935)
  blocking collectives: 670 us -> 591 us
  starting transfers between devices: 92.6 us -> 105 us
    all_gather x1 -> x0, blocking collectives: 77.2 us -> none  [per_device(): lax.all_gather(w_out, 'dp', axis=1, tiled=True)]
  transfers between devices with their start and end apart: 39 -> 40, of which waited for: 6 -> 6; matrix products, arithmetic and copies ran while one was open for 10% -> 11% of each run, Pallas kernels for 0% -> 0%
where the time goes in v1:
time: 1150 us; the launch traced here: 1140 us
  blocking collectives  591 us (51%)
  waiting for transfers between devices  273 us (24%)
  starting transfers between devices  105 us (9%)
  matrix products  65.9 us (6%)
  other arithmetic  48.6 us (4%)
  local copies, waits for them, and re-layouts  29 us (3%)
  between operations  17 us (1%)
    unnamed x1, blocking collectives  103 us
    all_gather x1, blocking collectives, per_device(): lax.all_gather(w_keyval, 'dp', axis=0, tiled=True)  86.8 us
    all_gather x1, blocking collectives, per_device(): lax.all_gather(w_gate, 'dp', axis=0, tiled=True)  86.1 us
    psum x1, blocking collectives, per_device(): lax.psum((keyval_part, gain_in_part, grad_gain_post_attn, grad_gain_pre_f...  82 us
    unnamed x30, starting transfers between devices  80.8 us
    all_gather x1, blocking collectives, per_device(): lax.all_gather(w_down, 'dp', axis=1, tiled=True)  79 us
    all_gather x1, blocking collectives, per_device(): lax.all_gather(w_up, 'dp', axis=0, tiled=True)  78.2 us
    psum x1, waiting for transfers between devices, per_device(): lax.psum((keyval_part, gain_in_part, grad_gain_post_attn, grad_gain_pre_f...  77.9 us
  transfers between devices with their start and end apart: 40, of which 6 were waited for; matrix products, arithmetic and copies ran while one was open for 11% of the time, Pallas kernels for 0%

profile of v1, /device:TPU:1, one launch (start us, length us, event | category | flops | bytes accessed | tf_op | source)
XLA Modules:
  0.0 1139.9 jit_solution(15518354489111897827)
XLA Ops:
  8.4 1.9 fusion.73
  11.8 11.5 %all-to-all-start = ((bf16[32,256,20]{1,2,0:T(8,128)(2,1)}), bf16[32,256,20]{1,2,0:T(8,128)(2,1)S(1)}, u32[]{:S(2)}, u32[]{:S(2)}) async-start(bf16[32,256,20]{1,2,0:T(8,128)(2,1)} %stack.2), calls=%async_computation | async-start | bytes 786432 | tf_op jit(solution)/shard_map/all_to_all | solution.py:102
  23.3 86.8 %all-gather.1 = bf16[32,20,512]{2,1,0:T(8,128)(2,1)S(1)} all-gather(bf16[1,20,512]{2,1,0:T(8,128)(2,1)S(1)} %bitcast.279), channel_id=1, replica_groups=mesh['dp'=32,'tensor'=4] {'dp'}, dimensions={0}, use_global_device_ids=true | all-gather | bytes 675840 | tf_op jit(solution)/shard_map/all_gather | solution.py:100
  110.2 75.5 %all-gather = bf16[32,20,256]{2,1,0:T(8,128)(2,1)S(1)} all-gather(bf16[1,20,256]{2,1,0:T(8,128)(2,1)S(1)} %bitcast.283), channel_id=1, replica_groups=mesh['dp'=32,'tensor'=4] {'dp'}, dimensions={0}, use_global_device_ids=true | all-gather | bytes 337920 | tf_op jit(solution)/shard_map/all_gather | solution.py:99
  188.7 2.5 fusion.103
  195.0 5.5 fusion.60
  204.0 14.0 %while.33 = (s32[]{:T(128)}, bf16[2,512,1,256]{3,1,2,0:T(8,128)(2,1)S(1)}, f32[2,1,512]{2,1,0:T(1,128)S(1)}, s32[2]{0:T(128)S(1)}, s32[1024]{0:T(1024)S(1)}, /*i...) while((s32[]{:T(128)}, ...), condition=%wide.region_8.9_spmd.clone, body=%wide.region_5.8_spmd.sunk.clone | while | flops 544211968 | bytes 8169671 | solution.py:141
  218.1 2.1 fusion.104
  220.3 58.0 %reduce-scatter.15.cloned.1.call-done = f32[256,640]{1,0:T(8,128)} async-done(((f32[1024,640]{1,0:T(8,128)}), f32[256,640]{1,0:T(8,128)}) %reduce-scatter.15.cloned.1.call-update) | async-done | bytes 655376 | tf_op jit(solution)/shard_map/reduce_scatter | solution.py:144
  281.9 86.1 %all-gather.2 = bf16[32,20,512]{2,1,0:T(8,128)(2,1)S(1)} all-gather(bf16[1,20,512]{2,1,0:T(8,128)(2,1)S(1)} %bitcast.280), channel_id=1, replica_groups=mesh['dp'=32,'tensor'=4] {'dp'}, dimensions={0}, use_global_device_ids=true | all-gather | bytes 675840 | tf_op jit(solution)/shard_map/all_gather | solution.py:153
  368.1 78.2 %all-gather.3 = bf16[32,20,512]{2,1,0:T(8,128)(2,1)S(1)} all-gather(bf16[1,20,512]{2,1,0:T(8,128)(2,1)S(1)} %bitcast.281), channel_id=1, replica_groups=mesh['dp'=32,'tensor'=4] {'dp'}, dimensions={0}, use_global_device_ids=true | all-gather | bytes 675840 | tf_op jit(solution)/shard_map/all_gather | solution.py:154
  447.4 79.0 %all-gather.4 = bf16[32,20,512]{2,1,0:T(8,128)(2,1)S(1)} all-gather(bf16[1,20,512]{2,1,0:T(8,128)(2,1)S(1)} %bitcast.282), channel_id=1, replica_groups=mesh['dp'=32,'tensor'=4] {'dp'}, dimensions={0}, use_global_device_ids=true | all-gather | bytes 675840 | tf_op jit(solution)/shard_map/all_gather | solution.py:155
  527.4 2.4 fusion.105
  529.8 2.6 multiply_convert_fusion.1
  533.5 2.5 fusion.106
  536.0 11.8 %all-gather.14.cloned.1.call-start = ((), (), s32[]{:S(2)}) async-start(), calls=%async_computation.9 | async-start | bytes 1638400 | tf_op jit(solution)/shard_map/all_gather | solution.py:171
  547.8 56.3 %reduce-scatter.17.cloned.1.call-done = f32[256,640]{1,0:T(8,128)} async-done(((f32[1024,640]{1,0:T(8,128)}), f32[256,640]{1,0:T(8,128)}) %reduce-scatter.17.cloned.1.call-update) | async-done | bytes 655376 | tf_op jit(solution)/shard_map/reduce_scatter | solution.py:162
  607.9 23.8 %all-gather.14.cloned.1.call-done = bf16[1024,640]{1,0:T(8,128)(2,1)} async-done(((bf16[256,640]{1,0:T(8,128)(2,1)}), bf16[1024,640]{1,0:T(8,128)(2,1)}) %all-gather.14.cloned.1.call-update) | async-done | bytes 1310736 | tf_op jit(solution)/shard_map/all_gather | solution.py:171
  631.8 5.2 multiply_convert_fusion
  638.5 2.5 convolution_add_fusion.1
  641.1 33.4 %reduce-scatter.19.cloned.1.call-done = f32[256,640]{1,0:T(8,128)} async-done(((f32[1024,640]{1,0:T(8,128)}), f32[256,640]{1,0:T(8,128)}) %reduce-scatter.19.cloned.1.call-update) | async-done | bytes 655376 | tf_op jit(solution)/shard_map/reduce_scatter | solution.py:180
  678.4 23.8 %all-gather.16.cloned.1.call-done = bf16[1024,640]{1,0:T(8,128)(2,1)} async-done(((bf16[256,640]{1,0:T(8,128)(2,1)}), bf16[1024,640]{1,0:T(8,128)(2,1)}) %all-gather.16.cloned.1.call-update) | async-done | bytes 1310736 | tf_op jit(solution)/shard_map/all_gather | solution.py:200
  702.2 2.7 fusion.46
  705.0 36.4 %while.34 = (s32[]{:T(128)}, f32[1024,256]{1,0:T(8,128)}, f32[1024,256]{1,0:T(8,128)}, f32[2,512,1,256]{3,1,2,0:T(8,128)}, s32[2]{0:T(128)S(1)}, /*index=5*/s32[...) while((s32[]{:T(128)}, f32[1024,256]{1,0:T(8,128)}, ...), condition=%wide.region_20.21_spmd.clone.clone, body=%wide.region_18.20_spmd.clone.sunk.clone | while | flops 1351484416 | bytes 46170532 | solution.py:234
  707.6 3.0 fusion.204
  712.0 3.0 fusion.205
  715.2 2.5 fusion.207
  720.3 2.5 convolution_add_fusion.5
  725.4 3.0 fusion.204
  729.8 3.0 fusion.205
  733.1 2.9 fusion.207
  738.5 2.9 convolution_add_fusion.5
  741.3 1.6 copy.65
  743.0 3.5 fusion.64
  746.6 4.1 fusion.67
  751.6 1.7 convolution_convert_fusion
  753.7 3.5 fusion.54
  757.3 4.1 multiply_reduce_fusion
  763.2 1.6 pad_maximum_fusion
  766.0 2.3 convolution_convert_fusion.1
  773.1 103.2 %fusion.97 = (bf16[24,256]{1,0:T(8,128)(2,1)S(1)}, bf16[256,24]{0,1:T(8,128)(2,1)S(1)}, bf16[24,512]{1,0:T(8,128)(2,1)S(1)}, bf16[24,512]{1,0:T(8,128)(2,1)S(1)}, bf16[512,24]{0,1:T(8,128)(2,1)S(1)}) fusion(bf16[640,256]{1,0:T(8,128)(2,1)S(1)} %convolution_convert_fusion.6, bf16[256,640]{0,1:T(8,128)(2,1)S(1)} %convolution_convert_fusion.5, ...), kind=kCustom, calls=%all-reduce-scatter.5 | all-reduce-scatter fusion | flops 1572865 | bytes 2720256
  878.9 4.9 collective-permute-start.17
  883.9 1.9 collective-permute-start.11
  885.8 4.8 collective-permute-start.5
  892.0 6.3 collective-permute-start.6
  898.3 3.2 collective-permute-start.7
  901.5 2.3 collective-permute-start.8
  903.8 5.3 collective-permute-start.9
  909.1 3.1 collective-permute-start
  912.2 2.5 collective-permute-start.1
  914.7 4.9 collective-permute-start.2
  919.7 1.9 collective-permute-start.3
  921.6 2.2 collective-permute-start.4
  925.4 5.2 collective-permute-start.25
  933.6 1.6 collective-permute-start.28
  937.4 2.2 collective-permute-start.18
  939.6 4.6 collective-permute-start.19
  947.2 1.7 collective-permute-start.22
  951.9 4.6 collective-permute-start.13
  956.5 1.9 collective-permute-start.14
  966.5 2.4 fusion.85
  968.9 1.7 fusion.74
  970.5 82.0 %all-reduce.14 = (f32[640]{0:T(1024)}, f32[640]{0:T(1024)}, f32[640]{0:T(1024)}, f32[640]{0:T(1024)}, f32[256]{0:T(256)}, /*index=5*/f32[256]{0:T(256)}) all-reduce(f32[640]{0:T(1024)S(1)} %get-tuple-element.396, f32[640]{0:T(1024)S(1)} %get-tuple-element.392, ...), channel_id=1, replica_groups=mesh['dp'=32,'tensor'=4] {'dp','tensor'}, use_global_device_ids=true, to_apply=%region_32.33 | all-reduce | flops 3072 | bytes 24576 | tf_op jit(solution)/shard_map/psum | solution.py:273
  1053.6 77.9 %all-reduce.18.cloned.1.call-done = f32[640,512]{1,0:T(8,128)} async-done(((f32[640,512]{1,0:T(8,128)}), f32[640,512]{1,0:T(8,128)}) %all-reduce.18.cloned.1.call-update) | async-done | bytes 1310736 | tf_op jit(solution)/shard_map/psum | solution.py:273
  (312 shorter events, 80.6 us)
Async XLA Ops:
  7.2 16.1 %copy-start.48 = (bf16[20,512]{1,0:T(8,128)(2,1)S(1)}, bf16[20,512]{1,0:T(8,128)(2,1)}, u32[]{:S(2)}) copy-start(bf16[20,512]{1,0:T(8,128)(2,1)} %param.23) | copy-start | bytes 61444
  7.2 181.5 %all-gather.10.cloned.1.call-start = ((), (), s32[]{:S(2)}) async-start(), calls=%async_computation.5 | async-start | bytes 1638400 | tf_op jit(solution)/shard_map/all_gather | solution.py:105
  8.4 101.9 %copy-start.56 = (bf16[20,256]{1,0:T(8,128)(2,1)S(1)}, bf16[20,256]{1,0:T(8,128)(2,1)}, u32[]{:S(2)}) copy-start(bf16[20,256]{1,0:T(8,128)(2,1)} %param.22) | copy-start | bytes 30724
  11.8 174.0 %copy-start.45 = (s32[1,1024]{1,0:T(1,128)S(1)}, s32[1,1024]{1,0:T(1,128)}, u32[]{:S(2)}) copy-start(s32[1,1024]{1,0:T(1,128)} %param.20) | copy-start | bytes 12292
  11.8 176.9 %all-to-all-start = ((bf16[32,256,20]{1,2,0:T(8,128)(2,1)}), bf16[32,256,20]{1,2,0:T(8,128)(2,1)S(1)}, u32[]{:S(2)}, u32[]{:S(2)}) async-start(bf16[32,256,20]{1,2,0:T(8,128)(2,1)} %stack.2), calls=%async_computation | async-start | bytes 786432 | tf_op jit(solution)/shard_map/all_to_all | solution.py:102
  23.2 255.1 %reduce-scatter.15.cloned.1.call-start = ((), (), s32[]{:S(2)}) async-start(), calls=%async_computation.6 | async-start | bytes 3276800 | tf_op jit(solution)/shard_map/reduce_scatter | solution.py:144
  110.2 81.1 %copy-start.24 = (bf16[640,512]{1,0:T(8,128)(2,1)}, bf16[640,512]{1,0:T(8,128)(2,1)S(1)}, u32[]{:S(2)}) copy-start(bf16[640,512]{1,0:T(8,128)(2,1)S(1)} %reshape.737) | copy-start | bytes 1966084
  185.8 6.0 copy-start.21
  188.7 29.4 %copy-start.23 = (bf16[256,640]{0,1:T(8,128)(2,1)}, bf16[256,640]{0,1:T(8,128)(2,1)S(1)}, u32[]{:S(2)}) copy-start(bf16[256,640]{0,1:T(8,128)(2,1)S(1)} %reshape.730) | copy-start | bytes 983044
  220.2 59.3 %copy-start.17 = (bf16[256,640]{1,0:T(8,128)(2,1)S(1)}, bf16[256,640]{1,0:T(8,128)(2,1)}, u32[]{:S(2)}) copy-start(bf16[256,640]{1,0:T(8,128)(2,1)} %param.19) | copy-start | bytes 983044
  220.2 59.3 %copy-start.47 = (f32[640]{0:T(1024)S(1)}, f32[640]{0:T(1024)}, u32[]{:S(2)}) copy-start(f32[640]{0:T(1024)} %param.29) | copy-start | bytes 7684
  220.2 60.8 %copy-start.46 = (f32[640]{0:T(1024)S(1)}, f32[640]{0:T(1024)}, u32[]{:S(2)}) copy-start(f32[640]{0:T(1024)} %param.30) | copy-start | bytes 7684
  220.2 61.6 %copy-start.49 = (bf16[20,512]{1,0:T(8,128)(2,1)S(1)}, bf16[20,512]{1,0:T(8,128)(2,1)}, u32[]{:S(2)}) copy-start(bf16[20,512]{1,0:T(8,128)(2,1)} %param.25) | copy-start | bytes 61444
  220.2 307.1 %all-gather.12.cloned.1.call-start = ((), (), s32[]{:S(2)}) async-start(), calls=%async_computation.7 | async-start | bytes 1638400 | tf_op jit(solution)/shard_map/all_gather | solution.py:157
  280.9 87.2 %copy-start.50 = (bf16[20,512]{1,0:T(8,128)(2,1)S(1)}, bf16[20,512]{1,0:T(8,128)(2,1)}, u32[]{:S(2)}) copy-start(bf16[20,512]{1,0:T(8,128)(2,1)} %param.26) | copy-start | bytes 61444
  281.8 322.3 %reduce-scatter.17.cloned.1.call-start = ((), (), s32[]{:S(2)}) async-start(), calls=%async_computation.8 | async-start | bytes 3276800 | tf_op jit(solution)/shard_map/reduce_scatter | solution.py:162
  281.9 165.5 %copy-start.51 = (bf16[512,20]{0,1:T(8,128)(2,1)S(1)}, bf16[512,20]{0,1:T(8,128)(2,1)}, u32[]{:S(2)}) copy-start(bf16[512,20]{0,1:T(8,128)(2,1)} %param.27) | copy-start | bytes 61444
  536.0 69.4 %copy-start.20 = (bf16[256,640]{1,0:T(8,128)(2,1)S(1)}, bf16[256,640]{1,0:T(8,128)(2,1)}, u32[]{:S(2)}) copy-start(bf16[256,640]{1,0:T(8,128)(2,1)} %param.21) | copy-start | bytes 983044
  536.0 69.4 %copy-start.52 = (f32[640]{0:T(1024)S(1)}, f32[640]{0:T(1024)}, u32[]{:S(2)}) copy-start(f32[640]{0:T(1024)} %param.31) | copy-start | bytes 7684
  536.0 95.8 %all-gather.14.cloned.1.call-start = ((), (), s32[]{:S(2)}) async-start(), calls=%async_computation.9 | async-start | bytes 1638400 | tf_op jit(solution)/shard_map/all_gather | solution.py:171
  607.9 66.6 %reduce-scatter.19.cloned.1.call-start = ((), (), s32[]{:S(2)}) async-start(), calls=%async_computation.10 | async-start | bytes 3276800 | tf_op jit(solution)/shard_map/reduce_scatter | solution.py:180
  641.1 34.7 %copy-start.6 = (f32[256,640]{1,0:T(8,128)S(1)}, f32[256,640]{1,0:T(8,128)}, u32[]{:S(2)}) copy-start(f32[256,640]{1,0:T(8,128)} %reduce-scatter.15.cloned.1.call-done) | copy-start | bytes 1966084
  641.1 61.1 %all-gather.16.cloned.1.call-start = ((), (), s32[]{:S(2)}) async-start(), calls=%async_computation.11 | async-start | bytes 1638400 | tf_op jit(solution)/shard_map/all_gather | solution.py:200
  677.3 27.7 %copy-start.11 = (f32[256,640]{1,0:T(8,128)}, f32[256,640]{1,0:T(8,128)S(1)}, u32[]{:S(2)}) copy-start(f32[256,640]{1,0:T(8,128)S(1)} %get-tuple-element.458) | copy-start | bytes 1966084
  677.3 27.7 %copy-start.43 = (bf16[1024,256]{1,0:T(8,128)(2,1)S(1)}, bf16[1024,256]{1,0:T(8,128)(2,1)}, u32[]{:S(2)}) copy-start(bf16[1024,256]{1,0:T(8,128)(2,1)} %copy-done.42) | copy-start | bytes 1572868
  678.3 288.2 %reduce-scatter.21.cloned.1.call-start = ((), (), s32[]{:S(2)}) async-start(), calls=%async_computation.12 | async-start | bytes 2949120 | tf_op jit(solution)/shard_map/reduce_scatter | solution.py:251
  705.0 10.0 copy-start.9
  722.8 10.0 copy-start.9
  764.9 366.7 %all-reduce.18.cloned.1.call-start = ((), (), s32[]{:S(2)}) async-start(), calls=%async_computation.13 | async-start | bytes 2621440 | tf_op jit(solution)/shard_map/psum | solution.py:273
  772.5 162.8 %copy-start.57 = (u32[128]{0:T(128)S(1)}, u32[128]{0:T(128)}, u32[]{:S(2)}) copy-start(u32[128]{0:T(128)} %constant.192) | copy-start | bytes 1540
  773.1 193.4 %copy-start.19 = (bf16[256,640]{1,0:T(8,128)(2,1)S(1)}, bf16[256,640]{1,0:T(8,128)(2,1)}, u32[]{:S(2)}) copy-start(bf16[256,640]{1,0:T(8,128)(2,1)} %fusion.73) | copy-start | bytes 983044
  876.3 22.0 %collective-permute-start.29 = (bf16[512,4]{0,1:T(4,128)(2,1)S(1)}, bf16[512,4]{0,1:T(4,128)(2,1)S(1)}, u32[]{:S(2)}, u32[]{:S(2)}) collective-permute-start(bf16[512,4]{0,1:T(4,128)(2,1)S(1)} %slice.73), channel_id=1, source_target_pairs={{0,24},{4,28},{8,32},{12,36},{16,40},{20,44},{24,48},{28,52},{32,5... | collective-permute-start | bytes 12296
  877.6 23.8 %collective-permute-start.23 = (bf16[4,512]{1,0:T(4,128)(2,1)S(1)}, bf16[4,512]{1,0:T(4,128)(2,1)S(1)}, u32[]{:S(2)}, u32[]{:S(2)}) collective-permute-start(bf16[4,512]{1,0:T(4,128)(2,1)S(1)} %slice.72), channel_id=1, source_target_pairs={{0,24},{4,28},{8,32},{12,36},{16,40},{20,44},{24,48},{28,52},{32,5... | collective-permute-start | bytes 12296
  878.9 24.8 %collective-permute-start.17 = (bf16[4,512]{1,0:T(4,128)(2,1)S(1)}, bf16[4,512]{1,0:T(4,128)(2,1)S(1)}, u32[]{:S(2)}, u32[]{:S(2)}) collective-permute-start(bf16[4,512]{1,0:T(4,128)(2,1)S(1)} %slice.71), channel_id=1, source_target_pairs={{0,24},{4,28},{8,32},{12,36},{16,40},{20,44},{24,48},{28,52},{32,5... | collective-permute-start | bytes 12296
  883.9 6.8 collective-permute-start.11
  885.8 6.1 collective-permute-start.5
  890.7 18.4 %collective-permute-start.10 = (bf16[256,24]{0,1:T(8,128)(2,1)S(1)}, bf16[256,24]{0,1:T(8,128)(2,1)S(1)}, u32[]{:S(2)}, u32[]{:S(2)}) collective-permute-start(bf16[256,24]{0,1:T(8,128)(2,1)S(1)} %get-tuple-element.452), channel_id=1, source_target_pairs={{0,20},{4,24},{8,28},{12,32},{16,36},{20,40},{24,44},{28,48},{32,5... | collective-permute-start | bytes 36872
  892.0 20.2 %collective-permute-start.6 = (bf16[256,24]{0,1:T(8,128)(2,1)S(1)}, bf16[256,24]{0,1:T(8,128)(2,1)S(1)}, u32[]{:S(2)}, u32[]{:S(2)}) collective-permute-start(bf16[256,24]{0,1:T(8,128)(2,1)S(1)} %get-tuple-element.452), channel_id=1, source_target_pairs={{0,4},{4,8},{8,12},{12,16},{16,20},{20,24},{24,28},{28,32},{32,36}... | collective-permute-start | bytes 36872
  898.3 16.4 %collective-permute-start.7 = (bf16[256,24]{0,1:T(8,128)(2,1)S(1)}, bf16[256,24]{0,1:T(8,128)(2,1)S(1)}, u32[]{:S(2)}, u32[]{:S(2)}) collective-permute-start(bf16[256,24]{0,1:T(8,128)(2,1)S(1)} %get-tuple-element.452), channel_id=1, source_target_pairs={{0,8},{4,12},{8,16},{12,20},{16,24},{20,28},{24,32},{28,36},{32,40... | collective-permute-start | bytes 36872
  901.5 18.2 %collective-permute-start.8 = (bf16[256,24]{0,1:T(8,128)(2,1)S(1)}, bf16[256,24]{0,1:T(8,128)(2,1)S(1)}, u32[]{:S(2)}, u32[]{:S(2)}) collective-permute-start(bf16[256,24]{0,1:T(8,128)(2,1)S(1)} %get-tuple-element.452), channel_id=1, source_target_pairs={{0,12},{4,16},{8,20},{12,24},{16,28},{20,32},{24,36},{28,40},{32,4... | collective-permute-start | bytes 36872
  903.8 17.8 %collective-permute-start.9 = (bf16[256,24]{0,1:T(8,128)(2,1)S(1)}, bf16[256,24]{0,1:T(8,128)(2,1)S(1)}, u32[]{:S(2)}, u32[]{:S(2)}) collective-permute-start(bf16[256,24]{0,1:T(8,128)(2,1)S(1)} %get-tuple-element.452), channel_id=1, source_target_pairs={{0,16},{4,20},{8,24},{12,28},{16,32},{20,36},{24,40},{28,44},{32,4... | collective-permute-start | bytes 36872
  909.1 14.7 %collective-permute-start = (bf16[24,256]{1,0:T(8,128)(2,1)S(1)}, bf16[24,256]{1,0:T(8,128)(2,1)S(1)}, u32[]{:S(2)}, u32[]{:S(2)}) collective-permute-start(bf16[24,256]{1,0:T(8,128)(2,1)S(1)} %get-tuple-element.451), channel_id=1, source_target_pairs={{0,4},{4,8},{8,12},{12,16},{16,20},{20,24},{24,28},{28,32},{32,36}... | collective-permute-start | bytes 36872
  912.2 13.2 %collective-permute-start.1 = (bf16[24,256]{1,0:T(8,128)(2,1)S(1)}, bf16[24,256]{1,0:T(8,128)(2,1)S(1)}, u32[]{:S(2)}, u32[]{:S(2)}) collective-permute-start(bf16[24,256]{1,0:T(8,128)(2,1)S(1)} %get-tuple-element.451), channel_id=1, source_target_pairs={{0,8},{4,12},{8,16},{12,20},{16,24},{20,28},{24,32},{28,36},{32,40... | collective-permute-start | bytes 36872
  914.7 16.0 %collective-permute-start.2 = (bf16[24,256]{1,0:T(8,128)(2,1)S(1)}, bf16[24,256]{1,0:T(8,128)(2,1)S(1)}, u32[]{:S(2)}, u32[]{:S(2)}) collective-permute-start(bf16[24,256]{1,0:T(8,128)(2,1)S(1)} %get-tuple-element.451), channel_id=1, source_target_pairs={{0,12},{4,16},{8,20},{12,24},{16,28},{20,32},{24,36},{28,40},{32,4... | collective-permute-start | bytes 36872
  919.7 12.4 %collective-permute-start.3 = (bf16[24,256]{1,0:T(8,128)(2,1)S(1)}, bf16[24,256]{1,0:T(8,128)(2,1)S(1)}, u32[]{:S(2)}, u32[]{:S(2)}) collective-permute-start(bf16[24,256]{1,0:T(8,128)(2,1)S(1)} %get-tuple-element.451), channel_id=1, source_target_pairs={{0,16},{4,20},{8,24},{12,28},{16,32},{20,36},{24,40},{28,44},{32,4... | collective-permute-start | bytes 36872
  921.6 12.0 %collective-permute-start.4 = (bf16[24,256]{1,0:T(8,128)(2,1)S(1)}, bf16[24,256]{1,0:T(8,128)(2,1)S(1)}, u32[]{:S(2)}, u32[]{:S(2)}) collective-permute-start(bf16[24,256]{1,0:T(8,128)(2,1)S(1)} %get-tuple-element.451), channel_id=1, source_target_pairs={{0,20},{4,24},{8,28},{12,32},{16,36},{20,40},{24,44},{28,48},{32,5... | collective-permute-start | bytes 36872
  923.8 13.6 %collective-permute-start.24 = (bf16[512,24]{0,1:T(8,128)(2,1)S(1)}, bf16[512,24]{0,1:T(8,128)(2,1)S(1)}, u32[]{:S(2)}, u32[]{:S(2)}) collective-permute-start(bf16[512,24]{0,1:T(8,128)(2,1)S(1)} %get-tuple-element.455), channel_id=1, source_target_pairs={{0,4},{4,8},{8,12},{12,16},{16,20},{20,24},{24,28},{28,32},{32,36}... | collective-permute-start | bytes 73736
  925.4 14.2 %collective-permute-start.25 = (bf16[512,24]{0,1:T(8,128)(2,1)S(1)}, bf16[512,24]{0,1:T(8,128)(2,1)S(1)}, u32[]{:S(2)}, u32[]{:S(2)}) collective-permute-start(bf16[512,24]{0,1:T(8,128)(2,1)S(1)} %get-tuple-element.455), channel_id=1, source_target_pairs={{0,8},{4,12},{8,16},{12,20},{16,24},{20,28},{24,32},{28,36},{32,40... | collective-permute-start | bytes 73736
  930.7 13.6 %collective-permute-start.26 = (bf16[512,24]{0,1:T(8,128)(2,1)S(1)}, bf16[512,24]{0,1:T(8,128)(2,1)S(1)}, u32[]{:S(2)}, u32[]{:S(2)}) collective-permute-start(bf16[512,24]{0,1:T(8,128)(2,1)S(1)} %get-tuple-element.455), channel_id=1, source_target_pairs={{0,12},{4,16},{8,20},{12,24},{16,28},{20,32},{24,36},{28,40},{32,4... | collective-permute-start | bytes 73736
  932.0 13.8 %collective-permute-start.27 = (bf16[512,24]{0,1:T(8,128)(2,1)S(1)}, bf16[512,24]{0,1:T(8,128)(2,1)S(1)}, u32[]{:S(2)}, u32[]{:S(2)}) collective-permute-start(bf16[512,24]{0,1:T(8,128)(2,1)S(1)} %get-tuple-element.455), channel_id=1, source_target_pairs={{0,16},{4,20},{8,24},{12,28},{16,32},{20,36},{24,40},{28,44},{32,4... | collective-permute-start | bytes 73736
  933.6 13.5 %collective-permute-start.28 = (bf16[512,24]{0,1:T(8,128)(2,1)S(1)}, bf16[512,24]{0,1:T(8,128)(2,1)S(1)}, u32[]{:S(2)}, u32[]{:S(2)}) collective-permute-start(bf16[512,24]{0,1:T(8,128)(2,1)S(1)} %get-tuple-element.455), channel_id=1, source_target_pairs={{0,20},{4,24},{8,28},{12,32},{16,36},{20,40},{24,44},{28,48},{32,5... | collective-permute-start | bytes 73736
  937.4 12.9 %collective-permute-start.18 = (bf16[24,512]{1,0:T(8,128)(2,1)S(1)}, bf16[24,512]{1,0:T(8,128)(2,1)S(1)}, u32[]{:S(2)}, u32[]{:S(2)}) collective-permute-start(bf16[24,512]{1,0:T(8,128)(2,1)S(1)} %get-tuple-element.454), channel_id=1, source_target_pairs={{0,4},{4,8},{8,12},{12,16},{16,20},{20,24},{24,28},{28,32},{32,36}... | collective-permute-start | bytes 73736
  939.6 12.3 %collective-permute-start.19 = (bf16[24,512]{1,0:T(8,128)(2,1)S(1)}, bf16[24,512]{1,0:T(8,128)(2,1)S(1)}, u32[]{:S(2)}, u32[]{:S(2)}) collective-permute-start(bf16[24,512]{1,0:T(8,128)(2,1)S(1)} %get-tuple-element.454), channel_id=1, source_target_pairs={{0,8},{4,12},{8,16},{12,20},{16,24},{20,28},{24,32},{28,36},{32,40... | collective-permute-start | bytes 73736
  944.3 12.3 %collective-permute-start.20 = (bf16[24,512]{1,0:T(8,128)(2,1)S(1)}, bf16[24,512]{1,0:T(8,128)(2,1)S(1)}, u32[]{:S(2)}, u32[]{:S(2)}) collective-permute-start(bf16[24,512]{1,0:T(8,128)(2,1)S(1)} %get-tuple-element.454), channel_id=1, source_target_pairs={{0,12},{4,16},{8,20},{12,24},{16,28},{20,32},{24,36},{28,40},{32,4... | collective-permute-start | bytes 73736
  945.9 12.6 %collective-permute-start.21 = (bf16[24,512]{1,0:T(8,128)(2,1)S(1)}, bf16[24,512]{1,0:T(8,128)(2,1)S(1)}, u32[]{:S(2)}, u32[]{:S(2)}) collective-permute-start(bf16[24,512]{1,0:T(8,128)(2,1)S(1)} %get-tuple-element.454), channel_id=1, source_target_pairs={{0,16},{4,20},{8,24},{12,28},{16,32},{20,36},{24,40},{28,44},{32,4... | collective-permute-start | bytes 73736
  947.2 12.6 %collective-permute-start.22 = (bf16[24,512]{1,0:T(8,128)(2,1)S(1)}, bf16[24,512]{1,0:T(8,128)(2,1)S(1)}, u32[]{:S(2)}, u32[]{:S(2)}) collective-permute-start(bf16[24,512]{1,0:T(8,128)(2,1)S(1)} %get-tuple-element.454), channel_id=1, source_target_pairs={{0,20},{4,24},{8,28},{12,32},{16,36},{20,40},{24,44},{28,48},{32,5... | collective-permute-start | bytes 73736
  950.3 13.3 %collective-permute-start.12 = (bf16[24,512]{1,0:T(8,128)(2,1)S(1)}, bf16[24,512]{1,0:T(8,128)(2,1)S(1)}, u32[]{:S(2)}, u32[]{:S(2)}) collective-permute-start(bf16[24,512]{1,0:T(8,128)(2,1)S(1)} %get-tuple-element.453), channel_id=1, source_target_pairs={{0,4},{4,8},{8,12},{12,16},{16,20},{20,24},{24,28},{28,32},{32,36}... | collective-permute-start | bytes 73736
  951.9 11.7 %collective-permute-start.13 = (bf16[24,512]{1,0:T(8,128)(2,1)S(1)}, bf16[24,512]{1,0:T(8,128)(2,1)S(1)}, u32[]{:S(2)}, u32[]{:S(2)}) collective-permute-start(bf16[24,512]{1,0:T(8,128)(2,1)S(1)} %get-tuple-element.453), channel_id=1, source_target_pairs={{0,8},{4,12},{8,16},{12,20},{16,24},{20,28},{24,32},{28,36},{32,40... | collective-permute-start | bytes 73736
  956.5 7.1 collective-permute-start.14
  958.5 5.1 collective-permute-start.15
  959.8 3.8 collective-permute-start.16
  962.6 6.2 copy-start.25
  962.7 6.2 copy-start.53
  968.8 83.8 %copy-start.12 = (f32[256,640]{1,0:T(8,128)S(1)}, f32[256,640]{1,0:T(8,128)}, u32[]{:S(2)}) copy-start(f32[256,640]{1,0:T(8,128)} %copy-done.11) | copy-start | bytes 1966084
  (43 other events, 95.8 us)
Sparse Core Ops, SparseCore 0:
  10.4 29.8 all-gather.9
  220.3 57.9 reduce-scatter.14
  281.9 24.7 all-gather.11
  536.1 67.9 reduce-scatter.16
  608.0 23.7 all-gather.13
  641.2 33.2 reduce-scatter.18
  678.4 23.7 all-gather.15
  765.0 35.7 reduce-scatter.20
  969.0 162.5 all-reduce.17
